TPU v7x, 1024 devices: a whole 4x8x16 slice. The times are simulated.
1024 devices in a mesh: group: 128 (over z, y), head: 8 (over x, core).
Axes of the slice: x: 4, y: 8, z: 16, core: 2. Of those that a mesh axis runs over, the one named last changes fastest.
Arguments:
- hidden_in: bfloat16 [3, 1024, 4096], P(None, 'group'), may hold values from -6 to 6
- norm_gain: float32 [4096], replicated, may hold values from 0.5 to 1.5
- w_gate_up: bfloat16 [128, 4096, 2, 1024], P('group', 'head'), may hold values from -0.09375 to 0.09375
- w_down: bfloat16 [128, 1024, 4096], P('group', None, 'head'), may hold values from -0.1875 to 0.1875
- route_ids: int32 [3, 1024, 8], P(None, 'group'), may hold values from 0 to 127, as said below
- route_weights: float32 [3, 1024, 8], P(None, 'group'), may hold values from 0.05 to 1
Outputs:
- mixed: bfloat16 [3, 1024, 4096], P(None, 'group', 'head')
Inputs may be any that keep to these rules, and one draw needn't show every extreme that they name: `route_ids`: in each micro-batch the 8 rows of one group name 8 different experts each, and no expert is named twice within that group and micro-batch.
All inputs are finite; a program needn't handle non-finite values.
Results may differ from a plain program's by a relative error of at most 0.012.
Values may be sent and summed in bfloat16 or wider, within the bound.
A program may use at most 32 MiB of HBM per device.

v0:
```python
import jax
import jax.numpy as jnp
from jax import lax
from jax.sharding import PartitionSpec as P


def per_device(hidden_in, norm_gain, w_gate_up, w_down, route_ids, route_weights):
    head_count = lax.axis_size("head")
    group_count = lax.axis_size("group")
    slice_width = hidden_in.shape[2] // head_count
    offset = lax.axis_index("head") * slice_width
    expert_number = jnp.arange(group_count, dtype=jnp.int32)
    gate_up = w_gate_up[0]
    down_proj = w_down[0]
    results = []
    for micro_batch in range(hidden_in.shape[0]):
        wide_tokens = hidden_in[micro_batch].astype(jnp.float32)
        scale = lax.rsqrt(jnp.mean(wide_tokens * wide_tokens, axis=-1, keepdims=True) + 1e-06)
        normed = (wide_tokens * scale * norm_gain).astype(jnp.bfloat16)
        own_slice = lax.dynamic_slice_in_dim(normed, offset, slice_width, 1)
        matches = route_ids[micro_batch][:, :, None] == expert_number[None, None, :]
        chosen = jnp.any(matches, axis=1).astype(jnp.bfloat16)
        outgoing = lax.dot_general(
            chosen, own_slice, (((0,), (0,)), ((), ())), preferred_element_type=jnp.float32
        ).astype(jnp.bfloat16)
        arrived = lax.all_to_all(outgoing, "group", split_axis=0, concat_axis=0, tiled=True)
        partial_value = jnp.einsum(
            "sw,wcf->scf", arrived, gate_up, preferred_element_type=jnp.float32
        )
        summed = lax.psum(partial_value.astype(jnp.bfloat16), "head").astype(jnp.float32)
        activated = (jax.nn.silu(summed[:, 0]) * summed[:, 1]).astype(jnp.bfloat16)
        expert_rows = jnp.dot(activated, down_proj, preferred_element_type=jnp.float32)
        returned = lax.all_to_all(
            expert_rows.astype(jnp.bfloat16), "group", split_axis=0, concat_axis=0, tiled=True
        )
        raw_weights = route_weights[micro_batch]
        gate_probs = raw_weights / jnp.sum(raw_weights, axis=-1, keepdims=True)
        mixing = jnp.sum(jnp.where(matches, gate_probs[:, :, None], jnp.float32(0.0)), axis=1)
        routed = jnp.dot(mixing, returned.astype(jnp.float32), precision=lax.Precision.HIGHEST)
        residual = lax.dynamic_slice_in_dim(wide_tokens, offset, slice_width, 1)
        results.append((residual + routed).astype(jnp.bfloat16))
    return jnp.stack(results)


def solution(mesh):
    in_specs = (
        P(None, "group", None),
        P(),
        P("group", "head", None, None),
        P("group", None, "head"),
        P(None, "group", None),
        P(None, "group", None),
    )
    out_specs = P(None, "group", "head")
    return jax.shard_map(
        per_device, mesh=mesh, in_specs=in_specs, out_specs=out_specs, check_vma=False
    )
```

profile of v0, /device:TPU:6, one launch (start us, length us, event | category | flops | bytes accessed | tf_op | source)
XLA Modules:
  0.0 278.0 jit_solution(15484194492573758335)
XLA Ops:
  6.5 1.2 multiply_reduce_fusion.2
  7.8 1.0 slice_convert_fusion.2
  8.7 0.7 slice_bitcast_fusion.2
  9.5 0.8 dynamic-slice.3
  12.5 26.3 %all-to-all-start.2 = ((bf16[128,2,256]{2,1,0:T(2,128)(2,1)}), bf16[128,2,256]{2,1,0:T(2,128)(2,1)S(1)}, u32[]{:S(2)}, u32[]{:S(2)}) async-start(bf16[128,2,256]{2,1,0:T(2,128)(2,1)} %reshape.119), calls=%async_computation.2 | async-start | bytes 262144 | tf_op jit(solution)/shard_map/all_to_all | solution.py:26
  39.0 0.7 reduce.3
  39.6 0.7 reshape.115
  40.3 16.1 %all-to-all-done.2 = bf16[128,2,256]{2,1,0:T(2,128)(2,1)S(1)} async-done(((bf16[128,2,256]{2,1,0:T(2,128)(2,1)}), bf16[128,2,256]{2,1,0:T(2,128)(2,1)S(1)}, u32[]{:S(2)}, u32[]{:S(2)}) %all-to-all-start.2) | async-done | bytes 131104 | tf_op jit(solution)/shard_map/all_to_all | solution.py:26
  56.5 6.6 %all-to-all-start.4 = ((bf16[128,2,256]{2,1,0:T(2,128)(2,1)}), bf16[128,2,256]{2,1,0:T(2,128)(2,1)S(1)}, u32[]{:S(2)}, u32[]{:S(2)}) async-start(bf16[128,2,256]{2,1,0:T(2,128)(2,1)} %reshape.115), calls=%async_computation.4 | async-start | bytes 262144 | tf_op jit(solution)/shard_map/all_to_all | solution.py:26
  63.4 0.7 reduce.5
  64.8 15.8 %all-to-all-done.4 = bf16[128,2,256]{2,1,0:T(2,128)(2,1)S(1)} async-done(((bf16[128,2,256]{2,1,0:T(2,128)(2,1)}), bf16[128,2,256]{2,1,0:T(2,128)(2,1)S(1)}, u32[]{:S(2)}, u32[]{:S(2)}) %all-to-all-start.4) | async-done | bytes 131104 | tf_op jit(solution)/shard_map/all_to_all | solution.py:26
  80.7 6.5 %all-to-all-start = ((bf16[128,2,256]{2,1,0:T(2,128)(2,1)}), bf16[128,2,256]{2,1,0:T(2,128)(2,1)S(1)}, u32[]{:S(2)}, u32[]{:S(2)}) async-start(bf16[128,2,256]{2,1,0:T(2,128)(2,1)} %reshape.123), calls=%async_computation | async-start | bytes 262144 | tf_op jit(solution)/shard_map/all_to_all | solution.py:26
  87.4 1.6 fusion.12
  89.0 1.6 fusion.9
  90.6 14.1 %all-to-all-done = bf16[128,2,256]{2,1,0:T(2,128)(2,1)S(1)} async-done(((bf16[128,2,256]{2,1,0:T(2,128)(2,1)}), bf16[128,2,256]{2,1,0:T(2,128)(2,1)S(1)}, u32[]{:S(2)}, u32[]{:S(2)}) %all-to-all-start) | async-done | bytes 131104 | tf_op jit(solution)/shard_map/all_to_all | solution.py:26
  104.8 1.6 fusion.6
  106.5 72.0 %all-reduce.3.cloned.1.call-done = (bf16[128,2,1024]{2,0,1:T(8,128)(2,1)}, bf16[128,2,1024]{2,0,1:T(8,128)(2,1)}, bf16[128,2,1024]{2,0,1:T(8,128)(2,1)}) async-done(((bf16[128,2,1024]{2,0,1:T(8,128)(2,1)}, bf16[128,2,1024]{2,0,1:T(8,128)(2,1)}, bf16[128,2,1024]{2,0,1:T(8,128)(2,1)}), (bf16[128,2,1024]{2,0,1:T(8,128)(2,1)}, bf16[128,2,1024]{2,0,1:T(8,128)(2,1)}, ...) | async-done | bytes 1572880 | tf_op jit(solution)/shard_map/psum | solution.py:30
  178.5 1.1 convert_element_type.121
  179.7 1.6 fusion.17
  181.3 0.7 reduce.6
  182.0 0.7 reshape.117
  182.6 19.6 %all-to-all-start.5 = ((bf16[128,2,256]{2,1,0:T(2,128)(2,1)}), bf16[128,2,256]{2,1,0:T(2,128)(2,1)S(1)}, u32[]{:S(2)}, u32[]{:S(2)}) async-start(bf16[128,2,256]{2,1,0:T(2,128)(2,1)} %reshape.117), calls=%async_computation.5 | async-start | bytes 262144 | tf_op jit(solution)/shard_map/all_to_all | solution.py:33
  202.4 1.6 fusion.16
  204.0 0.7 reduce.7
  204.7 0.7 reshape.121
  205.4 14.2 %all-to-all-done.5 = bf16[128,2,256]{2,1,0:T(2,128)(2,1)S(1)} async-done(((bf16[128,2,256]{2,1,0:T(2,128)(2,1)}), bf16[128,2,256]{2,1,0:T(2,128)(2,1)S(1)}, u32[]{:S(2)}, u32[]{:S(2)}) %all-to-all-start.5) | async-done | bytes 131104 | tf_op jit(solution)/shard_map/all_to_all | solution.py:33
  219.6 8.4 %all-to-all-start.3 = ((bf16[128,2,256]{2,1,0:T(2,128)(2,1)}), bf16[128,2,256]{2,1,0:T(2,128)(2,1)S(1)}, u32[]{:S(2)}, u32[]{:S(2)}) async-start(bf16[128,2,256]{2,1,0:T(2,128)(2,1)} %reshape.121), calls=%async_computation.3 | async-start | bytes 262144 | tf_op jit(solution)/shard_map/all_to_all | solution.py:33
  228.3 1.6 fusion.15
  229.9 0.7 reduce.8
  231.2 14.8 %all-to-all-done.3 = bf16[128,2,256]{2,1,0:T(2,128)(2,1)S(1)} async-done(((bf16[128,2,256]{2,1,0:T(2,128)(2,1)}), bf16[128,2,256]{2,1,0:T(2,128)(2,1)S(1)}, u32[]{:S(2)}, u32[]{:S(2)}) %all-to-all-start.3) | async-done | bytes 131104 | tf_op jit(solution)/shard_map/all_to_all | solution.py:33
  246.0 6.6 %all-to-all-start.1 = ((bf16[128,2,256]{2,1,0:T(2,128)(2,1)}), bf16[128,2,256]{2,1,0:T(2,128)(2,1)S(1)}, u32[]{:S(2)}, u32[]{:S(2)}) async-start(bf16[128,2,256]{2,1,0:T(2,128)(2,1)} %reshape.125), calls=%async_computation.1 | async-start | bytes 262144 | tf_op jit(solution)/shard_map/all_to_all | solution.py:33
  253.4 16.8 %all-to-all-done.1 = bf16[128,2,256]{2,1,0:T(2,128)(2,1)S(1)} async-done(((bf16[128,2,256]{2,1,0:T(2,128)(2,1)}), bf16[128,2,256]{2,1,0:T(2,128)(2,1)S(1)}, u32[]{:S(2)}, u32[]{:S(2)}) %all-to-all-start.1) | async-done | bytes 131104 | tf_op jit(solution)/shard_map/all_to_all | solution.py:33
  (38 shorter events, 6.6 us)
Async XLA Ops:
  6.5 80.8 %copy-start = (bf16[1,512,2,1024]{3,2,1,0:T(2,128)(2,1)S(1)}, bf16[1,512,2,1024]{3,2,1,0:T(2,128)(2,1)}, u32[]{:S(2)}) copy-start(bf16[1,512,2,1024]{3,2,1,0:T(2,128)(2,1)} %param.8) | copy-start | bytes 6291460
  12.5 44.0 %all-to-all-start.2 = ((bf16[128,2,256]{2,1,0:T(2,128)(2,1)}), bf16[128,2,256]{2,1,0:T(2,128)(2,1)S(1)}, u32[]{:S(2)}, u32[]{:S(2)}) async-start(bf16[128,2,256]{2,1,0:T(2,128)(2,1)} %reshape.119), calls=%async_computation.2 | async-start | bytes 262144 | tf_op jit(solution)/shard_map/all_to_all | solution.py:26
  56.5 24.2 %all-to-all-start.4 = ((bf16[128,2,256]{2,1,0:T(2,128)(2,1)}), bf16[128,2,256]{2,1,0:T(2,128)(2,1)S(1)}, u32[]{:S(2)}, u32[]{:S(2)}) async-start(bf16[128,2,256]{2,1,0:T(2,128)(2,1)} %reshape.115), calls=%async_computation.4 | async-start | bytes 262144 | tf_op jit(solution)/shard_map/all_to_all | solution.py:26
  80.7 24.0 %all-to-all-start = ((bf16[128,2,256]{2,1,0:T(2,128)(2,1)}), bf16[128,2,256]{2,1,0:T(2,128)(2,1)S(1)}, u32[]{:S(2)}, u32[]{:S(2)}) async-start(bf16[128,2,256]{2,1,0:T(2,128)(2,1)} %reshape.123), calls=%async_computation | async-start | bytes 262144 | tf_op jit(solution)/shard_map/all_to_all | solution.py:26
  87.2 91.3 %all-reduce.3.cloned.1.call-start = ((), (), s32[]{:S(2)}) async-start(), calls=%async_computation.6 | async-start | bytes 3145728 | tf_op jit(solution)/shard_map/psum | solution.py:30
  179.6 22.6 %copy-start.2 = (bf16[128,2,1024]{2,0,1:T(8,128)(2,1)S(1)}, bf16[128,2,1024]{2,0,1:T(8,128)(2,1)}, u32[]{:S(2)}) copy-start(bf16[128,2,1024]{2,0,1:T(8,128)(2,1)} %get-tuple-element.12) | copy-start | bytes 1572868
  182.6 36.9 %all-to-all-start.5 = ((bf16[128,2,256]{2,1,0:T(2,128)(2,1)}), bf16[128,2,256]{2,1,0:T(2,128)(2,1)S(1)}, u32[]{:S(2)}, u32[]{:S(2)}) async-start(bf16[128,2,256]{2,1,0:T(2,128)(2,1)} %reshape.117), calls=%async_computation.5 | async-start | bytes 262144 | tf_op jit(solution)/shard_map/all_to_all | solution.py:33
  202.3 25.7 %copy-start.3 = (f32[3,8,8]{2,1,0:T(8,128)S(1)}, f32[3,8,8]{2,1,0:T(8,128)}, u32[]{:S(2)}) copy-start(f32[3,8,8]{2,1,0:T(8,128)} %param.11) | copy-start | bytes 2308
  202.3 25.8 %copy-start.1 = (bf16[128,2,1024]{2,0,1:T(8,128)(2,1)S(1)}, bf16[128,2,1024]{2,0,1:T(8,128)(2,1)}, u32[]{:S(2)}) copy-start(bf16[128,2,1024]{2,0,1:T(8,128)(2,1)} %get-tuple-element.13) | copy-start | bytes 1572868
  219.6 26.4 %all-to-all-start.3 = ((bf16[128,2,256]{2,1,0:T(2,128)(2,1)}), bf16[128,2,256]{2,1,0:T(2,128)(2,1)S(1)}, u32[]{:S(2)}, u32[]{:S(2)}) async-start(bf16[128,2,256]{2,1,0:T(2,128)(2,1)} %reshape.121), calls=%async_computation.3 | async-start | bytes 262144 | tf_op jit(solution)/shard_map/all_to_all | solution.py:33
  246.0 24.2 %all-to-all-start.1 = ((bf16[128,2,256]{2,1,0:T(2,128)(2,1)}), bf16[128,2,256]{2,1,0:T(2,128)(2,1)S(1)}, u32[]{:S(2)}, u32[]{:S(2)}) async-start(bf16[128,2,256]{2,1,0:T(2,128)(2,1)} %reshape.125), calls=%async_computation.1 | async-start | bytes 262144 | tf_op jit(solution)/shard_map/all_to_all | solution.py:33
Sparse Core Ops, SparseCore 0:
  106.6 71.8 all-reduce.2
where the time goes:
time: 279 us; the launch traced here: 278 us
  waiting for transfers between devices  164 us (59%)
  starting transfers between devices  73.9 us (26%)
  between operations  13.7 us (5%)
  matrix products  11 us (4%)
  other arithmetic  8.84 us (3%)
  local copies, waits for them, and re-layouts  6.7 us (2%)
    psum x1, waiting for transfers between devices, per_device(): lax.psum(partial_value.astype(jnp.bfloat16), 'head').astype(jnp.float32)  72 us
    all_to_all x3, waiting for transfers between devices, per_device(): lax.all_to_all(outgoing, 'group', split_axis=0, concat_axis=0, tiled=True)  46 us
    all_to_all x3, waiting for transfers between devices, per_device(): lax.all_to_all(expert_rows.astype(jnp.bfloat16), 'group', split_axis=0, c...  45.9 us
    all_to_all x3, starting transfers between devices, per_device(): lax.all_to_all(outgoing, 'group', split_axis=0, concat_axis=0, tiled=True)  39.3 us
    all_to_all x3, starting transfers between devices, per_device(): lax.all_to_all(expert_rows.astype(jnp.bfloat16), 'group', split_axis=0, c...  34.5 us
  transfers between devices with their start and end apart: 7, of which 7 were waited for; matrix products, arithmetic and copies ran while one was open for 5% of the time, Pallas kernels for 0%

commit v1 on v0

v1 whole, which is shorter than its diff:
```python
import functools

import jax
import jax.numpy as jnp
from jax import lax
from jax.experimental import pallas as pl
from jax.experimental.pallas import tpu as pltpu
from jax.sharding import PartitionSpec as P

MESH = pl.DeviceIdType.MESH
F32 = jnp.float32
BF16 = jnp.bfloat16
NEAR = 4
CORES = 2
META = 16


class Copies:
    def __init__(self, send_sem, recv_sem):
        self.send_sem, self.recv_sem = send_sem, recv_sem
        self.all = []

    def start(self, src, dst, device):
        i = len(self.all)
        copy = pltpu.make_async_remote_copy(
            src_ref=src,
            dst_ref=dst,
            send_sem=self.send_sem.at[i],
            recv_sem=self.recv_sem.at[i],
            device_id=device,
            device_id_type=MESH,
        )
        copy.start()
        self.all.append(copy)
        return copy


def copy_count(dims):
    nz, ny, nx, mb = dims
    far, near, along_y, along_x = nz // NEAR - 1, 4, ny - 1, nx - 1
    return (far + near) + mb * 2 * (far + near + along_y + along_x + 1)


def kernel(
    dims, h_ref, gain_ref, ids_ref, weights_ref, gate_up_hbm, down_hbm, out_ref,
    raw, gate_up, down, meta, meta_t, mixing, rows, slots, arrived, terms, core_in, pair_sum,
    x_in, activated, expert_out, returned, partial, near_in, z_sum, far_in,
    load_sem, send_sem, recv_sem,
):
    nz, ny, nx, mb = dims
    far = nz // NEAR
    head_count = nx * CORES
    width = rows.shape[-1] * 2
    half_width = width // 2
    ff = activated.shape[-1]
    topk = ids_ref.shape[-1]
    group = lax.axis_index("group")
    head = lax.axis_index("head")
    z, y = lax.div(group, ny), lax.rem(group, ny)
    x, core = lax.div(head, CORES), lax.rem(head, CORES)
    residue, block = lax.rem(z, NEAR), lax.div(z, NEAR)
    place = residue * far + block
    share = core * nx + x

    load_gate_up = pltpu.make_async_copy(gate_up_hbm.at[0], raw, load_sem.at[0])
    load_down = pltpu.make_async_copy(down_hbm.at[0], down, load_sem.at[1])
    load_gate_up.start()
    load_down.start()

    def at_z(step):
        return {"group": lax.rem(z + step + nz, nz) * ny + y, "head": head}

    def at_y(other):
        return {"group": z * ny + other, "head": head}

    def at_x(other):
        return {"group": group, "head": other * CORES + core}

    other_core = {"group": group, "head": x * CORES + (1 - core)}
    far_steps = [NEAR * k for k in range(1, far)]
    peers = [at_z(s) for s in far_steps + [1, -1, 2, -2]]
    peers += [at_y(lax.rem(y + k, ny)) for k in range(1, ny)]
    peers += [at_x(lax.rem(x + k, nx)) for k in range(1, nx)]
    peers += [other_core]
    barrier = pltpu.get_barrier_semaphore()
    for peer in peers:
        pl.semaphore_signal(barrier, inc=1, device_id=peer, device_id_type=MESH)

    copies = Copies(send_sem, recv_sem)
    pending = {}

    def landed(name):
        for copy in pending.pop(name):
            copy.wait_recv()

    column = pl.multiple_of(head * width, 128)

    lane = lax.broadcasted_iota(jnp.int32, (8, 128), 1)
    tile = jnp.zeros((8, 128), F32)
    for m in range(mb):
        ids = ids_ref[m].astype(F32)
        raw_weights = weights_ref[m]
        probs = raw_weights / jnp.sum(raw_weights, axis=-1, keepdims=True)
        for k in range(topk):
            tile = jnp.where(lane == META * m + k, ids[:, k : k + 1], tile)
            tile = jnp.where(lane == META * m + 8 + k, probs[:, k : k + 1], tile)
    meta[place] = tile

    def norm(m):
        wide = h_ref[m].astype(F32)
        scale = lax.rsqrt(jnp.mean(wide * wide, axis=-1, keepdims=True) + 1e-06)
        own = h_ref[m, :, pl.ds(column, width)].astype(F32)
        chunks = width // 128
        gain = jnp.concatenate([gain_ref[pl.ds(head * chunks + j, 1), :] for j in range(chunks)], axis=1)
        normed = own * scale * gain
        rows[m, place] = jnp.concatenate([normed[:, :half_width], normed[:, half_width:]], axis=0).astype(BF16)

    def gather_far(m):
        if m == 0:
            pending["meta far"] = [copies.start(meta.at[place], meta.at[place], at_z(s)) for s in far_steps]
        block_ref = rows.at[m, place]
        pending["far", m] = [copies.start(block_ref, block_ref, at_z(s)) for s in far_steps]

    def near_copies(ref):
        whole = ref.at[pl.ds(residue * far, far)]
        low = ref.at[pl.ds(residue * far, far // 2)]
        high = ref.at[pl.ds(residue * far + far // 2, far // 2)]
        return [
            copies.start(part, part, at_z(step)) for part, step in ((whole, 1), (whole, -1), (low, 2), (high, -2))
        ]

    def gather_near(m):
        if m == 0:
            landed("meta far")
            pending["meta near"] = near_copies(meta)
        landed(("far", m))
        pending["near", m] = near_copies(rows.at[m])

    quads = nz * 16
    lane_q = lax.broadcasted_iota(jnp.int32, (nz, quads), 1)
    slot_p = lax.broadcasted_iota(jnp.int32, (nz, quads), 0)
    same_group = slot_p == lax.div(lane_q, 16)
    first_half = lax.rem(lax.div(lax.broadcasted_iota(jnp.int32, (ny * nz, quads), 1), 8), 2) == 0

    def routing(m, values):
        out = []
        ids = meta_t[META * m : META * m + 8, :]
        probs = meta_t[META * m + 8 : META * m + 16, :]
        valid = lax.broadcasted_iota(jnp.int32, ids.shape, 0) < topk
        for other in range(ny):
            match = jnp.logical_and(ids == (z * ny + other).astype(F32), valid)
            picked = jnp.where(match, probs if values else 1.0, 0.0)
            found = jnp.sum(picked, axis=0, keepdims=True)
            out.append(jnp.where(same_group, found, 0.0))
        return jnp.concatenate(out, axis=0)

    def dispatch(m):
        landed(("near", m))
        if m == 0:
            landed("meta near")
            own = meta[...]
            twice = jnp.concatenate([own, own], axis=1).reshape(quads, 128)
            meta_t[...] = twice.T
        chosen = routing(m, False)
        source = rows[m].reshape(quads, half_width)
        for half in range(2):
            pick = jnp.where(first_half if half == 0 else jnp.logical_not(first_half), chosen, 0.0).astype(BF16)
            got = jnp.dot(pick, source, preferred_element_type=F32).astype(BF16)
            slots[m, :, :, half * half_width : (half + 1) * half_width] = got.reshape(ny, nz, half_width)
        pending["y", m] = send_y(slots.at[m], arrived.at[m])
        arrived[m, y] = slots[m, y]

    def send_y(source, target):
        started = []
        for k in range(1, ny):
            other = lax.rem(y + k, ny)
            started.append(copies.start(source.at[other], target.at[y], at_y(other)))
        return started

    def mix_weights(m):
        gates = routing(m, True)
        for half in range(2):
            keep = jnp.where(first_half if half == 0 else jnp.logical_not(first_half), gates, 0.0)
            mixing[m, half] = keep.T.astype(BF16)

    def expert_in(m):
        landed(("y", m))
        block_in = arrived[m].reshape(ny * nz, width)
        step = min(256, ff)
        for part in range(2):
            for start in range(0, ff, step):
                got = jnp.dot(block_in, gate_up[part, :, start : start + step], preferred_element_type=F32)
                at = part * ff + start
                terms[m, :, :, at : at + step] = got.astype(BF16).reshape(ny, nz, step)
        pending["core", m] = [
            copies.start(terms.at[m, pl.ds((1 - core) * nx, nx)], core_in.at[m], other_core)
        ]

    def pair(m):
        landed(("core", m))
        total = terms[m, pl.ds(core * nx, nx)].astype(F32) + core_in[m].astype(F32)
        pair_sum[m] = total.astype(BF16)
        pending["x", m] = []
        for k in range(1, nx):
            other = lax.rem(x + k, nx)
            pending["x", m].append(copies.start(pair_sum.at[m, other], x_in.at[m, k - 1], at_x(other)))

    def activate(m):
        landed(("x", m))
        total = pair_sum[m, x].astype(F32)
        for k in range(nx - 1):
            total = total + x_in[m, k].astype(F32)
        gate, up = total[:, :ff], total[:, ff:]
        activated[m, share] = (gate / (1.0 + jnp.exp(-gate)) * up).astype(BF16)
        own = activated.at[m, share]
        pending["x back", m] = [
            copies.start(own, own, at_x(lax.rem(x + k, nx))) for k in range(1, nx)
        ]

    def share_pair(m):
        landed(("x back", m))
        own = activated.at[m, pl.ds(core * nx, nx)]
        pending["core back", m] = [copies.start(own, own, other_core)]

    def expert_back(m):
        landed(("core back", m))
        got = jnp.dot(activated[m].reshape(ny * nz, ff), down[...], preferred_element_type=F32)
        expert_out[m] = got.astype(BF16).reshape(ny, nz, width)
        pending["y back", m] = send_y(expert_out.at[m], returned.at[m])
        returned[m, y] = expert_out[m, y]

    def mix(m):
        landed(("y back", m))
        back = returned[m].reshape(ny * nz, width)
        got = jnp.dot(mixing[m, 0], back[:, :half_width], preferred_element_type=F32)
        got = got + jnp.dot(mixing[m, 1], back[:, half_width:], preferred_element_type=F32)
        partial[m] = got.astype(BF16).reshape(nz, 16, half_width)
        source = partial.at[m]

        def of(cls, first, count):
            return source.at[pl.ds(lax.rem(residue + cls, NEAR) * far + first, count)]

        pending["near back", m] = [
            copies.start(of(1, 0, far), near_in.at[m, 0], at_z(1)),
            copies.start(of(3, 0, far), near_in.at[m, 1], at_z(-1)),
            copies.start(of(2, 0, far // 2), near_in.at[m, 2, pl.ds(0, far // 2)], at_z(2)),
            copies.start(of(2, far // 2, far // 2), near_in.at[m, 2, pl.ds(far // 2, far // 2)], at_z(-2)),
        ]

    def reduce_near(m):
        landed(("near back", m))
        total = partial[m, pl.ds(residue * far, far)].astype(F32)
        for k in range(3):
            total = total + near_in[m, k].astype(F32)
        z_sum[m] = total.astype(BF16)
        pending["far back", m] = []
        for k in range(1, far):
            other = lax.rem(block + k, far)
            pending["far back", m].append(
                copies.start(z_sum.at[m, other], far_in.at[m, k - 1], at_z(NEAR * k))
            )

    def finish(m):
        landed(("far back", m))
        total = z_sum[m, block].astype(F32)
        for k in range(far - 1):
            total = total + far_in[m, k].astype(F32)
        residual = h_ref[m, :, pl.ds(column, width)].astype(F32)
        out_ref[m, :, :half_width] = (residual[:, :half_width] + total[:8]).astype(BF16)
        out_ref[m, :, half_width:] = (residual[:, half_width:] + total[8:]).astype(BF16)

    step = 16
    steps = width // step

    def unpack(first, last):
        def body(i, carry):
            at = pl.ds(pl.multiple_of(i * step, step), step)
            both = raw[at].astype(F32)
            gate_up[0, at, :] = both[:, 0, :].astype(BF16)
            gate_up[1, at, :] = both[:, 1, :].astype(BF16)
            return carry

        lax.fori_loop(first, last, body, 0)

    batches = range(mb)
    for m in batches:
        norm(m)
        if m == 0:
            pl.semaphore_wait(barrier, len(peers))
        gather_far(m)
    load_gate_up.wait()
    unpack(0, steps // 4)
    for m in batches:
        gather_near(m)
    unpack(steps // 4, steps // 2)
    for m in batches:
        dispatch(m)
    unpack(steps // 2, steps)
    load_down.wait()
    for m in batches:
        expert_in(m)
    for m in batches:
        mix_weights(m)
    for stage in (pair, activate, share_pair, expert_back, mix, reduce_near, finish):
        for m in batches:
            stage(m)
    for copy in copies.all:
        copy.wait_send()


def per_device(dims, hidden_in, norm_gain, w_gate_up, w_down, route_ids, route_weights):
    nz, ny, nx, mb = dims
    far = nz // NEAR
    width, ff = w_gate_up.shape[1], w_gate_up.shape[3]
    vmem = pl.BlockSpec(memory_space=pltpu.VMEM)
    hbm = pl.BlockSpec(memory_space=pl.ANY)
    count = copy_count(dims)
    scratch = [
        pltpu.VMEM((width, 2, ff), BF16),
        pltpu.VMEM((2, width, ff), BF16),
        pltpu.VMEM((ff, width), BF16),
        pltpu.VMEM((nz, 8, 128), F32),
        pltpu.VMEM((128, nz * 16), F32),
        pltpu.VMEM((mb, 2, nz * 16, ny * nz), BF16),
        pltpu.VMEM((mb, nz, 16, width // 2), BF16),
        pltpu.VMEM((mb, ny, nz, width), BF16),
        pltpu.VMEM((mb, ny, nz, width), BF16),
        pltpu.VMEM((mb, ny, nz, 2 * ff), BF16),
        pltpu.VMEM((mb, nx, nz, 2 * ff), BF16),
        pltpu.VMEM((mb, nx, nz, 2 * ff), BF16),
        pltpu.VMEM((mb, max(nx - 1, 1), nz, 2 * ff), BF16),
        pltpu.VMEM((mb, ny, nz, ff), BF16),
        pltpu.VMEM((mb, ny, nz, width), BF16),
        pltpu.VMEM((mb, ny, nz, width), BF16),
        pltpu.VMEM((mb, nz, 16, width // 2), BF16),
        pltpu.VMEM((mb, 3, far, 16, width // 2), BF16),
        pltpu.VMEM((mb, far, 16, width // 2), BF16),
        pltpu.VMEM((mb, far - 1, 16, width // 2), BF16),
        pltpu.SemaphoreType.DMA((2,)),
        pltpu.SemaphoreType.DMA((count,)),
        pltpu.SemaphoreType.DMA((count,)),
    ]
    return pl.pallas_call(
        functools.partial(kernel, dims),
        out_shape=jax.ShapeDtypeStruct((mb, hidden_in.shape[1], width), BF16),
        in_specs=[vmem, vmem, vmem, vmem, hbm, hbm],
        out_specs=vmem,
        scratch_shapes=scratch,
        compiler_params=pltpu.CompilerParams(
            collective_id=0, has_side_effects=True, vmem_limit_bytes=44 << 20
        ),
    )(hidden_in, norm_gain.reshape(-1, 128), route_ids, route_weights, w_gate_up, w_down)


def solution(mesh, ny=8):
    group_count, head_count = mesh.shape["group"], mesh.shape["head"]

    def run(hidden_in, norm_gain, w_gate_up, w_down, route_ids, route_weights):
        dims = (group_count // ny, ny, head_count // CORES, hidden_in.shape[0])
        return jax.shard_map(
            functools.partial(per_device, dims),
            mesh=mesh,
            in_specs=(
                P(None, "group", None),
                P(),
                P("group", "head", None, None),
                P("group", None, "head"),
                P(None, "group", None),
                P(None, "group", None),
            ),
            out_specs=P(None, "group", "head"),
            check_vma=False,
        )(hidden_in, norm_gain, w_gate_up, w_down, route_ids, route_weights)

    return run
```

time: 279 us -> 93.5 us (0.34)
  the two profiles are of different devices: /device:TPU:6 before, /device:TPU:24 now
where the time goes in v1:
time: 93.5 us; the launch traced here: 93.2 us
  Pallas kernels  86.7 us (93%)
  local copies, waits for them, and re-layouts  6.48 us (7%)
    pallas_call x1, Pallas kernels, per_device(): pl.pallas_call(functools.partial(kernel, dims), out_shape=jax.ShapeDtypeS...  86.7 us
    unnamed x13, local copies, waits for them, and re-layouts  6.48 us

profile of v1, /device:TPU:24, one launch (start us, length us, event | category | flops | bytes accessed | tf_op | source)
XLA Modules:
  0.0 93.2 jit_solution(13565907885180736923)
XLA Ops:
  0.0 0.0 copy-start
  0.0 1.6 %copy-done = bf16[1,512,2,1024]{3,2,1,0:T(2,128)(2,1)S(1)} copy-done((bf16[1,512,2,1024]{3,2,1,0:T(2,128)(2,1)S(1)}, bf16[1,512,2,1024]{3,2,1,0:T(2,128)(2,1)}, u32[]{:S(2)}) %copy-start) | copy-done | bytes 2097176
  1.6 0.0 copy-start.1
  1.6 1.2 %copy-done.1 = bf16[1,1024,512]{2,1,0:T(8,128)(2,1)S(1)} copy-done((bf16[1,1024,512]{2,1,0:T(8,128)(2,1)S(1)}, bf16[1,1024,512]{2,1,0:T(8,128)(2,1)}, u32[]{:S(2)}) %copy-start.1) | copy-done | bytes 1048600
  2.8 0.0 copy-start.2
  2.8 0.9 copy-done.2
  3.7 0.0 copy-start.3
  3.7 0.7 copy-done.3
  4.5 0.0 copy-start.4
  4.5 0.7 copy-done.4
  5.2 0.0 copy-start.5
  5.2 0.7 copy-done.5
  5.9 86.7 %shard_map.64 = bf16[3,8,512]{2,1,0:T(8,128)(2,1)S(1)} custom-call(bf16[3,8,4096]{2,1,0:T(8,128)(2,1)S(1)} %copy-done.2, f32[32,128]{1,0:T(8,128)S(1)} %bitcast.1, s32[3,8,8]{2,1,0:T(8,128)S(1)} %copy-done.4, f32[3,8,8]{2,1,0:T(8,128)S(1)} %copy-done.5, bf16[1,512,2,1024]{3,2,1,0:T(2,128)(2,1)S(1)} %copy-done, bf16[1,1024,512]{2,1,0:T(8,128)(2,1)S(1)} %copy-done.1), custom_call_target="tpu_custom_call" | custom-call | tf_op jit(solution)/shard_map/pallas_call | solution.py:343
  92.5 0.6 copy.8
Async XLA Ops:
  0.0 1.6 %copy-start = (bf16[1,512,2,1024]{3,2,1,0:T(2,128)(2,1)S(1)}, bf16[1,512,2,1024]{3,2,1,0:T(2,128)(2,1)}, u32[]{:S(2)}) copy-start(bf16[1,512,2,1024]{3,2,1,0:T(2,128)(2,1)} %gate_up_hbm.1) | copy-start | bytes 6291460
  1.6 1.2 %copy-start.1 = (bf16[1,1024,512]{2,1,0:T(8,128)(2,1)S(1)}, bf16[1,1024,512]{2,1,0:T(8,128)(2,1)}, u32[]{:S(2)}) copy-start(bf16[1,1024,512]{2,1,0:T(8,128)(2,1)} %down_hbm.1) | copy-start | bytes 3145732
  2.8 0.9 copy-start.2
  3.7 0.7 copy-start.3
  4.5 0.7 copy-start.4
  5.2 0.7 copy-start.5

commit v2 on v1

v2 whole, which is shorter than its diff:
```python
import functools

import jax
import jax.numpy as jnp
from jax import lax
from jax.experimental import pallas as pl
from jax.experimental.pallas import tpu as pltpu
from jax.sharding import PartitionSpec as P

MESH = pl.DeviceIdType.MESH
F32 = jnp.float32
BF16 = jnp.bfloat16
NEAR = 2
CORES = 2
META = 16


class Copies:
    def __init__(self, send_sem, recv_sem):
        self.send_sem, self.recv_sem = send_sem, recv_sem
        self.all = []

    def start(self, src, dst, device):
        i = len(self.all)
        copy = pltpu.make_async_remote_copy(
            src_ref=src,
            dst_ref=dst,
            send_sem=self.send_sem.at[i],
            recv_sem=self.recv_sem.at[i],
            device_id=device,
            device_id_type=MESH,
        )
        copy.start()
        self.all.append(copy)
        return copy


def copy_count(dims):
    nz, ny, nx, mb = dims
    far, to_slots = nz // NEAR - 1, NEAR * ny - 1
    return far + mb * 2 * (far + to_slots + (nx - 1) + 1)


def kernel(
    dims, h_hbm, gain_hbm, ids_hbm, weights_hbm, gate_up_hbm, down_hbm, out_ref,
    h_ref, gain_ref, ids_ref, weights_ref, raw, gate_up, down, meta, meta_t, mixing, rows, slots, arrived, terms, core_in, pair_sum,
    x_in, activated, expert_out, returned, partial, far_in,
    load_sem, send_sem, recv_sem,
):
    nz, ny, nx, mb = dims
    far = nz // NEAR
    head_count = nx * CORES
    width = rows.shape[-1] * 2
    half_width = width // 2
    ff = activated.shape[-1]
    topk = ids_ref.shape[-1]
    group = lax.axis_index("group")
    head = lax.axis_index("head")
    z, y = lax.div(group, ny), lax.rem(group, ny)
    x, core = lax.div(head, CORES), lax.rem(head, CORES)
    block = lax.div(z, NEAR)
    toward = 1 - 2 * core
    share = core * nx + x

    load_gate_up = pltpu.make_async_copy(gate_up_hbm.at[0], raw, load_sem.at[0])
    load_down = pltpu.make_async_copy(down_hbm.at[0], down, load_sem.at[1])
    load_small = [
        pltpu.make_async_copy(source, target, load_sem.at[2 + i])
        for i, (source, target) in enumerate(
            ((ids_hbm, ids_ref), (weights_hbm, weights_ref), (gain_hbm, gain_ref), (h_hbm, h_ref))
        )
    ]
    for load in load_small:
        load.start()
    load_gate_up.start()
    load_down.start()

    def at_z(step):
        return {"group": lax.rem(z + step + nz, nz) * ny + y, "head": head}

    def at_zy(step, other):
        return {"group": lax.rem(z + step + nz, nz) * ny + other, "head": head}

    def at_x(other):
        return {"group": group, "head": other * CORES + core}

    other_core = {"group": group, "head": x * CORES + (1 - core)}
    far_order = sorted(range(1, far), key=lambda k: -min(k, far - k))
    y_order = sorted(range(1, ny), key=lambda k: -min(k, ny - k))
    others_y = [lax.rem(y + k, ny) for k in y_order] + [y]
    peers = [at_z(NEAR * k) for k in far_order]
    peers += [at_zy(0, other) for other in others_y[:-1]]
    peers += [at_zy(side, other) for side in (1, -1) for other in others_y]
    peers += [at_x(lax.rem(x + k, nx)) for k in range(1, nx)]
    peers += [other_core]
    barrier = pltpu.get_barrier_semaphore()
    for peer in peers:
        pl.semaphore_signal(barrier, inc=1, device_id=peer, device_id_type=MESH)

    copies = Copies(send_sem, recv_sem)
    pending = {}

    def landed(name):
        for copy in pending.pop(name):
            copy.wait_recv()

    column = pl.multiple_of(head * width, 128)
    for load in load_small:
        load.wait()

    lane = lax.broadcasted_iota(jnp.int32, (8, 128), 1)
    tile = jnp.zeros((8, 128), F32)
    for m in range(mb):
        ids = ids_ref[m].astype(F32)
        raw_weights = weights_ref[m]
        probs = raw_weights / jnp.sum(raw_weights, axis=-1, keepdims=True)
        for k in range(topk):
            tile = jnp.where(lane == META * m + k, ids[:, k : k + 1], tile)
            tile = jnp.where(lane == META * m + 8 + k, probs[:, k : k + 1], tile)
    meta[block] = tile

    def norm(m):
        wide = h_ref[m].astype(F32)
        scale = lax.rsqrt(jnp.mean(wide * wide, axis=-1, keepdims=True) + 1e-06)
        own = h_ref[m, :, pl.ds(column, width)].astype(F32)
        chunks = width // 128
        gain = jnp.concatenate([gain_ref[pl.ds(head * chunks + j, 1), :] for j in range(chunks)], axis=1)
        normed = own * scale * gain
        rows[m, block] = jnp.concatenate([normed[:, :half_width], normed[:, half_width:]], axis=0).astype(BF16)

    def gather(m):
        if m == 0:
            own = meta.at[block]
            pending["meta"] = [copies.start(own, own, at_z(NEAR * k)) for k in far_order]
        own_rows = rows.at[m, block]
        pending["far", m] = [copies.start(own_rows, own_rows, at_z(NEAR * k)) for k in far_order]

    quads = far * 16
    lane_q = lax.broadcasted_iota(jnp.int32, (2 * far, quads), 1)
    slot_row = lax.broadcasted_iota(jnp.int32, (2 * far, quads), 0)
    same_block = lax.rem(slot_row, far) == lax.div(lane_q, 16)
    same_half = lax.div(slot_row, far) == lax.rem(lax.div(lane_q, 8), 2)
    same = jnp.logical_and(same_block, same_half)

    def routing(m, values):
        out = []
        ids = meta_t[META * m : META * m + 8, :]
        probs = meta_t[META * m + 8 : META * m + 16, :]
        valid = lax.broadcasted_iota(jnp.int32, ids.shape, 0) < topk
        for side in range(NEAR):
            first = lax.rem(z + toward * side + nz, nz) * ny
            for other in range(ny):
                match = jnp.logical_and(ids == (first + other).astype(F32), valid)
                picked = jnp.where(match, probs if values else 1.0, 0.0)
                found = jnp.sum(picked, axis=0, keepdims=True)
                out.append(jnp.where(same, found, 0.0))
        return jnp.concatenate(out, axis=0)

    def dispatch(m):
        if m == 0:
            landed("meta")
            own = meta[...]
            twice = jnp.concatenate([own, own], axis=1).reshape(quads, 128)
            meta_t[...] = twice.T
        pick = routing(m, False).astype(BF16)
        landed(("far", m))
        got = jnp.dot(pick, rows[m].reshape(quads, half_width), preferred_element_type=F32)
        slots[m] = got.astype(BF16).reshape(NEAR, ny, 2 * far, half_width)
        pending["slots", m] = exchange(slots.at[m], arrived.at[m], toward)
        arrived[m, 0, y] = slots[m, 0, y]

    def exchange(source, target, direction):
        started = []
        for i, other in enumerate(others_y):
            for side in (1, 0):
                if side == 1 or i < ny - 1:
                    device = at_zy(direction * side, other)
                    started.append(copies.start(source.at[side, other], target.at[side, y], device))
        return started

    def mix_weights(m):
        mixing[m] = routing(m, True).T.astype(BF16)

    def expert_in(m):
        landed(("slots", m))
        folded = arrived[m].astype(F32).reshape(NEAR * ny, 2 * far, half_width)
        halves = [folded[:, h * far : (h + 1) * far].reshape(ny * nz, half_width) for h in range(2)]
        block_in = jnp.concatenate(halves, axis=1).astype(BF16)
        step = min(256, ff)
        for part in range(2):
            for start in range(0, ff, step):
                got = jnp.dot(block_in, gate_up[part, :, start : start + step], preferred_element_type=F32)
                at = part * ff + start
                terms[m, :, :, at : at + step] = got.astype(BF16).reshape(ny, nz, step)
        pending["core", m] = [
            copies.start(terms.at[m, pl.ds((1 - core) * nx, nx)], core_in.at[m], other_core)
        ]

    def pair(m):
        landed(("core", m))
        total = terms[m, pl.ds(core * nx, nx)].astype(F32) + core_in[m].astype(F32)
        pair_sum[m] = total.astype(BF16)
        pending["x", m] = []
        for k in range(1, nx):
            other = lax.rem(x + k, nx)
            pending["x", m].append(copies.start(pair_sum.at[m, other], x_in.at[m, k - 1], at_x(other)))

    def activate(m):
        landed(("x", m))
        total = pair_sum[m, x].astype(F32)
        for k in range(nx - 1):
            total = total + x_in[m, k].astype(F32)
        gate, up = total[:, :ff], total[:, ff:]
        activated[m, share] = (gate / (1.0 + jnp.exp(-gate)) * up).astype(BF16)
        own = activated.at[m, share]
        pending["x back", m] = [
            copies.start(own, own, at_x(lax.rem(x + k, nx))) for k in range(1, nx)
        ]

    def share_pair(m):
        landed(("x back", m))
        own = activated.at[m, pl.ds(core * nx, nx)]
        pending["core back", m] = [copies.start(own, own, other_core)]

    def expert_back(m):
        landed(("core back", m))
        got = jnp.dot(activated[m].reshape(ny * nz, ff), down[...], preferred_element_type=F32)
        got = got.reshape(NEAR * ny, far, width)
        folded = jnp.concatenate([got[:, :, :half_width], got[:, :, half_width:]], axis=1)
        expert_out[m] = folded.astype(BF16).reshape(NEAR, ny, 2 * far, half_width)
        pending["slots back", m] = exchange(expert_out.at[m], returned.at[m], -toward)
        returned[m, 0, y] = expert_out[m, 0, y]

    def mix(m):
        landed(("slots back", m))
        back = returned[m].reshape(NEAR * ny * 2 * far, half_width)
        got = jnp.dot(mixing[m], back, preferred_element_type=F32)
        partial[m] = got.astype(BF16).reshape(far, 16, half_width)
        pending["far back", m] = []
        for k in far_order:
            other = lax.rem(block + k, far)
            pending["far back", m].append(
                copies.start(partial.at[m, other], far_in.at[m, k - 1], at_z(NEAR * k))
            )

    def finish(m):
        landed(("far back", m))
        total = partial[m, block].astype(F32)
        for k in range(far - 1):
            total = total + far_in[m, k].astype(F32)
        residual = h_ref[m, :, pl.ds(column, width)].astype(F32)
        out_ref[m, :, :half_width] = (residual[:, :half_width] + total[:8]).astype(BF16)
        out_ref[m, :, half_width:] = (residual[:, half_width:] + total[8:]).astype(BF16)

    step = 16
    steps = width // step

    def unpack():
        def body(i, carry):
            at = pl.ds(pl.multiple_of(i * step, step), step)
            both = raw[at].astype(F32)
            gate_up[0, at, :] = both[:, 0, :].astype(BF16)
            gate_up[1, at, :] = both[:, 1, :].astype(BF16)
            return carry

        lax.fori_loop(0, steps, body, 0)

    batches = range(mb)
    for m in batches:
        norm(m)
        if m == 0:
            pl.semaphore_wait(barrier, len(peers))
        gather(m)
    load_gate_up.wait()
    unpack()
    load_down.wait()
    for m in batches:
        dispatch(m)
    for m in batches:
        mix_weights(m)
    due = ((expert_in, 15), (pair, 17.5), (activate, 22), (share_pair, 26), (expert_back, 27.5), (mix, 32), (finish, 38))
    order = sorted((at + 3 * m, m, i) for i, (_, at) in enumerate(due) for m in batches)
    for _, m, i in order:
        due[i][0](m)
    for copy in copies.all:
        copy.wait_send()


def per_device(dims, hidden_in, norm_gain, w_gate_up, w_down, route_ids, route_weights):
    nz, ny, nx, mb = dims
    far = nz // NEAR
    width, ff = w_gate_up.shape[1], w_gate_up.shape[3]
    vmem = pl.BlockSpec(memory_space=pltpu.VMEM)
    hbm = pl.BlockSpec(memory_space=pltpu.HBM)
    count = copy_count(dims)
    gain = norm_gain.reshape(-1, 128)
    scratch = [
        *(pltpu.VMEM(a.shape, a.dtype) for a in (hidden_in, gain, route_ids, route_weights)),
        pltpu.VMEM((width, 2, ff), BF16),
        pltpu.VMEM((2, width, ff), BF16),
        pltpu.VMEM((ff, width), BF16),
        pltpu.VMEM((far, 8, 128), F32),
        pltpu.VMEM((128, far * 16), F32),
        pltpu.VMEM((mb, far * 16, NEAR * ny * 2 * far), BF16),
        pltpu.VMEM((mb, far, 16, width // 2), BF16),
        pltpu.VMEM((mb, NEAR, ny, 2 * far, width // 2), BF16),
        pltpu.VMEM((mb, NEAR, ny, 2 * far, width // 2), BF16),
        pltpu.VMEM((mb, ny, nz, 2 * ff), BF16),
        pltpu.VMEM((mb, nx, nz, 2 * ff), BF16),
        pltpu.VMEM((mb, nx, nz, 2 * ff), BF16),
        pltpu.VMEM((mb, max(nx - 1, 1), nz, 2 * ff), BF16),
        pltpu.VMEM((mb, ny, nz, ff), BF16),
        pltpu.VMEM((mb, NEAR, ny, 2 * far, width // 2), BF16),
        pltpu.VMEM((mb, NEAR, ny, 2 * far, width // 2), BF16),
        pltpu.VMEM((mb, far, 16, width // 2), BF16),
        pltpu.VMEM((mb, far - 1, 16, width // 2), BF16),
        pltpu.SemaphoreType.DMA((6,)),
        pltpu.SemaphoreType.DMA((count,)),
        pltpu.SemaphoreType.DMA((count,)),
    ]
    return pl.pallas_call(
        functools.partial(kernel, dims),
        out_shape=jax.ShapeDtypeStruct((mb, hidden_in.shape[1], width), BF16),
        in_specs=[hbm] * 6,
        out_specs=vmem,
        scratch_shapes=scratch,
        compiler_params=pltpu.CompilerParams(
            collective_id=0, has_side_effects=True, vmem_limit_bytes=60 << 20
        ),
    )(hidden_in, gain, route_ids, route_weights, w_gate_up, w_down)


def solution(mesh, ny=8):
    group_count, head_count = mesh.shape["group"], mesh.shape["head"]

    def run(hidden_in, norm_gain, w_gate_up, w_down, route_ids, route_weights):
        dims = (group_count // ny, ny, head_count // CORES, hidden_in.shape[0])
        return jax.shard_map(
            functools.partial(per_device, dims),
            mesh=mesh,
            in_specs=(
                P(None, "group", None),
                P(),
                P("group", "head", None, None),
                P("group", None, "head"),
                P(None, "group", None),
                P(None, "group", None),
            ),
            out_specs=P(None, "group", "head"),
            check_vma=False,
        )(hidden_in, norm_gain, w_gate_up, w_down, route_ids, route_weights)

    return run
```

time: 93.5 us -> 79.3 us (0.85)
  the two profiles are of different devices: /device:TPU:24 before, /device:TPU:1 now
where the time goes in v2:
time: 79.3 us; the launch traced here: 79.1 us
  Pallas kernels  77.8 us (98%)
  local copies, waits for them, and re-layouts  1.35 us (2%)
    pallas_call x1, Pallas kernels, per_device(): pl.pallas_call(functools.partial(kernel, dims), out_shape=jax.ShapeDtypeS...  77.8 us

profile of v2, /device:TPU:1, one launch (start us, length us, event | category | flops | bytes accessed | tf_op | source)
XLA Modules:
  0.0 79.1 jit_solution(2498352052693566121)
XLA Ops:
  0.0 77.8 %shard_map.64 = bf16[3,8,512]{2,1,0:T(8,128)(2,1)} custom-call(bf16[3,8,4096]{2,1,0:T(8,128)(2,1)} %h_hbm.1, f32[32,128]{1,0:T(8,128)} %bitcast.1, s32[3,8,8]{2,1,0:T(8,128)} %ids_hbm.1, f32[3,8,8]{2,1,0:T(8,128)} %weights_hbm.1, bf16[1,512,2,1024]{3,2,1,0:T(2,128)(2,1)} %gate_up_hbm.1, bf16[1,1024,512]{2,1,0:T(8,128)(2,1)} %down_hbm.1), custom_call_target="tpu_custom_call" | custom-call | tf_op jit(solution)/shard_map/pallas_call | solution.py:321
  77.8 1.3 %copy.8 = bf16[3,8,512]{2,1,0:T(8,128)(2,1)} copy(bf16[3,8,512]{2,1,0:T(8,128)(2,1)} %shard_map.64) | data formatting | bytes 49152

commit v3 on v2

--- a/solution.py
+++ b/solution.py
@@ -268,8 +268,8 @@
     batches = range(mb)
     for m in batches:
         norm(m)
-        if m == 0:
-            pl.semaphore_wait(barrier, len(peers))
+    pl.semaphore_wait(barrier, len(peers))
+    for m in batches:
         gather(m)
     load_gate_up.wait()
     unpack()
@@ -320,7 +320,7 @@
     ]
     return pl.pallas_call(
         functools.partial(kernel, dims),
-        out_shape=jax.ShapeDtypeStruct((mb, hidden_in.shape[1], width), BF16),
+        out_shape=pltpu.VMEM((mb, hidden_in.shape[1], width), BF16),
         in_specs=[hbm] * 6,
         out_specs=vmem,
         scratch_shapes=scratch,

time: 79.3 us -> 77.9 us (0.982)
  no operation moved by 1% of the time
where the time goes in v3:
time: 77.9 us; the launch traced here: 77.7 us
  Pallas kernels  77.1 us (99%)
    pallas_call x1, Pallas kernels, per_device(): pl.pallas_call(functools.partial(kernel, dims), out_shape=pltpu.VMEM((mb,...  77.1 us

profile of v3, /device:TPU:1, one launch (start us, length us, event | category | flops | bytes accessed | tf_op | source)
XLA Modules:
  0.0 77.7 jit_solution(9991663684560084946)
XLA Ops:
  0.0 77.1 %shard_map.64 = bf16[3,8,512]{2,1,0:T(8,128)(2,1)S(1)} custom-call(bf16[3,8,4096]{2,1,0:T(8,128)(2,1)} %h_hbm.1, f32[32,128]{1,0:T(8,128)} %bitcast.1, s32[3,8,8]{2,1,0:T(8,128)} %ids_hbm.1, f32[3,8,8]{2,1,0:T(8,128)} %weights_hbm.1, bf16[1,512,2,1024]{3,2,1,0:T(2,128)(2,1)} %gate_up_hbm.1, bf16[1,1024,512]{2,1,0:T(8,128)(2,1)} %down_hbm.1), custom_call_target="tpu_custom_call" | custom-call | tf_op jit(solution)/shard_map/pallas_call | solution.py:321
  77.1 0.6 copy.8
